TPU v7x, 256 devices: a whole 4x4x8 slice. The times are simulated.
256 devices in a mesh: dp: 32 (over y_hi, z, core), panel: 4 (over x), bin: 2 (over y_lo).
Axes of the slice: x: 4, y: 4 (y_hi: 2, y_lo: 2; y = y_hi * 2 + y_lo), z: 8, core: 2. Of those that a mesh axis runs over, the one named last changes fastest.
Arguments:
- histograms: bfloat16 [393216, 256], P('dp', 'bin'), may hold values from -6 to 6
- first_assign: int32 [393216], P('dp'), may hold values from 0 to 1023
- second_assign: int32 [393216], P('dp'), may hold values from 0 to 1023
- start_centroids: float32 [1024, 256], P('panel', 'bin'), may hold values from -3 to 3
Outputs:
- centroids: float32 [1024, 256], P('panel', 'bin')
- distortion: float32 [393216], P(('dp', 'bin'))
All inputs are finite; a program needn't handle non-finite values.
Results may differ from a plain program's by a relative error of at most 0.0015.
Values may be sent and summed in bfloat16 or wider, within the bound.
A program may use at most 64 MiB of HBM per device.

v0:
```python
import jax
import jax.numpy as jnp
from jax import lax
from jax.sharding import PartitionSpec as P


def on_device(histograms, first_assign, second_assign, start_centroids):
    panel_rows = start_centroids.shape[0]
    dp_count = lax.axis_size("dp")
    total_buckets = panel_rows * lax.axis_size("panel")
    prior = histograms.shape[0] * dp_count // total_buckets
    panel_start = lax.axis_index("panel") * panel_rows
    bucket_ids = panel_start + jnp.arange(panel_rows, dtype=jnp.int32)

    def lloyd_update(previous, assign):
        onehot = (assign[:, None] == bucket_ids[None, :]).astype(jnp.bfloat16)
        sums = lax.dot_general(
            onehot, histograms, (((0,), (0,)), ((), ())), preferred_element_type=jnp.float32
        )
        counts = jnp.sum(onehot, axis=0, dtype=jnp.float32)
        sums, counts = lax.psum((sums, counts), "dp")
        return (sums + prior * previous) / (counts + prior)[:, None]

    middle = lloyd_update(start_centroids, first_assign)
    centroids = lloyd_update(middle, second_assign)
    full_rows = lax.all_to_all(histograms, "bin", split_axis=0, concat_axis=1, tiled=True)
    full_cent = lax.all_gather(centroids.astype(jnp.bfloat16), "bin", axis=1, tiled=True).astype(
        centroids.dtype
    )
    norms = jnp.sum(full_cent * full_cent, axis=1)
    dots = jnp.dot(full_rows, full_cent.astype(jnp.bfloat16).T, preferred_element_type=jnp.float32)
    local_least = jnp.min(norms[None, :] - 2.0 * dots, axis=1)
    distortion = lax.pmin(local_least, "panel")
    return (centroids, distortion)


def solution(mesh):
    return jax.shard_map(
        on_device,
        mesh=mesh,
        in_specs=(P("dp", "bin"), P("dp"), P("dp"), P("panel", "bin")),
        out_specs=(P("panel", "bin"), P(("dp", "bin"))),
        check_vma=False,
    )
```

profile of v0, /device:TPU:1, one launch (start us, length us, event | category | flops | bytes accessed | tf_op | source)
XLA Modules:
  0.0 325.4 jit_solution(2826202792336550718)
XLA Ops:
  7.2 0.0 copy-start.2
  7.2 4.1 %all-to-all-start = ((bf16[2,6144,128]{2,1,0:T(8,128)(2,1)}), bf16[2,6144,128]{2,1,0:T(8,128)(2,1)S(1)}, u32[]{:S(2)}, u32[]{:S(2)}) async-start(bf16[2,6144,128]{2,1,0:T(8,128)(2,1)} %bitcast.8), calls=%async_computation | async-start | bytes 6291456 | tf_op jit(solution)/shard_map/all_to_all | solution.py:26
  11.3 0.0 all-reduce.4.cloned.1.call-start
  11.3 0.0 copy-done.2
  11.3 0.0 copy-start
  11.4 0.0 copy-start.3
  11.4 7.8 %fusion = f32[256,128]{1,0:T(8,128)} fusion(bf16[12288,128]{1,0:T(8,128)(2,1)} %param.4, s32[256]{0:T(256)S(1)} %iota_add_fusion, s32[12288]{0:T(1024)S(1)} %copy-done.2), kind=kOutput, calls=%fused_computation.1 | convolution fusion | flops 808452096 | bytes 3326976 | tf_op jit(solution)/shard_map/dot_general | solution.py:17
  19.2 0.0 copy-done
  19.2 0.0 copy-done.3
  19.2 0.0 copy-start.1
  19.2 5.7 %fusion.2 = f32[256,128]{1,0:T(8,128)} fusion(bf16[12288,128]{1,0:T(8,128)(2,1)S(1)} %copy-done, s32[256]{0:T(256)S(1)} %iota_add_fusion, s32[12288]{0:T(1024)S(1)} %copy-done.3), kind=kOutput, calls=%fused_computation.4 | convolution fusion | flops 808452096 | bytes 3326976 | tf_op jit(solution)/shard_map/dot_general | solution.py:17
  24.9 0.0 all-reduce.4.cloned.1.call-update
  24.9 7.0 %convert_reduce_fusion.1 = (f32[256]{0:T(256)S(1)}, f32[256]{0:T(256)S(1)}) fusion(s32[256]{0:T(256)S(1)} %iota_add_fusion, s32[12288]{0:T(1024)S(1)} %copy-done.2, s32[12288]{0:T(1024)S(1)} %copy-done.3), kind=kLoop, calls=%fused_computation.7 | loop fusion | flops 25165312 | bytes 101376 | tf_op jit(solution)/shard_map/reduce_sum | solution.py:20
  32.0 69.3 %all-reduce = (f32[256]{0:T(256)S(1)}, f32[256]{0:T(256)S(1)}) all-reduce(f32[256]{0:T(256)S(1)} %get-tuple-element.3, f32[256]{0:T(256)S(1)} %get-tuple-element.2), channel_id=1, replica_groups=mesh['dp'=32,'panel'=4,'bin'=2] {'dp'}, use_global_device_ids=true, to_apply=%region_5.0 | all-reduce | flops 512 | bytes 4096 | tf_op jit(solution)/shard_map/psum | solution.py:21
  101.3 192.0 %all-reduce.4.cloned.1.call-done = (f32[256,128]{1,0:T(8,128)}, f32[256,128]{1,0:T(8,128)}) async-done(((f32[256,128]{1,0:T(8,128)}, f32[256,128]{1,0:T(8,128)}), (f32[256,128]{1,0:T(8,128)}, f32[256,128]{1,0:T(8,128)})) %all-reduce.4.cloned.1.call-update) | async-done | bytes 262160 | tf_op jit(solution)/shard_map/psum | solution.py:21
  293.3 0.0 copy-done.1
  293.3 1.8 fusion.10
  295.1 3.8 %all_gather.3 = bf16[256,256]{1,0:T(8,128)(2,1)S(1)} all-gather(bf16[256,128]{1,0:T(8,128)(2,1)S(1)} %get-tuple-element.8), channel_id=1, replica_groups=mesh['dp'=32,'panel'=4,'bin'=2] {'bin'}, dimensions={1}, use_global_device_ids=true | all-gather | bytes 196608 | tf_op jit(solution)/shard_map/all_gather | solution.py:27
  298.9 0.1 multiply_reduce_fusion
  299.0 0.0 all-to-all-done
  299.0 2.8 copy.7
  301.9 2.9 fusion.9
  304.8 13.8 %pmin.7 = f32[6144]{0:T(1024)} all-reduce(f32[6144]{0:T(1024)S(1)} %fusion.9), channel_id=1, replica_groups=mesh['dp'=32,'panel'=4,'bin'=2] {'panel'}, use_global_device_ids=true, to_apply=%region_8.0 | all-reduce | flops 6144 | bytes 49152 | tf_op jit(solution)/shard_map/pmin | solution.py:33
  (2 shorter events, 0.0 us)
Async XLA Ops:
  7.2 4.2 %copy-start.2 = (s32[12288]{0:T(1024)S(1)}, s32[12288]{0:T(1024)}, u32[]{:S(2)}) copy-start(s32[12288]{0:T(1024)} %param.5) | copy-start | bytes 147460
  7.2 291.9 %all-to-all-start = ((bf16[2,6144,128]{2,1,0:T(8,128)(2,1)}), bf16[2,6144,128]{2,1,0:T(8,128)(2,1)S(1)}, u32[]{:S(2)}, u32[]{:S(2)}) async-start(bf16[2,6144,128]{2,1,0:T(8,128)(2,1)} %bitcast.8), calls=%async_computation | async-start | bytes 6291456 | tf_op jit(solution)/shard_map/all_to_all | solution.py:26
  11.3 282.1 %all-reduce.4.cloned.1.call-start = ((), (), s32[]{:S(2)}) async-start(), calls=%async_computation.1 | async-start | bytes 524288 | tf_op jit(solution)/shard_map/psum | solution.py:21
  11.3 7.8 %copy-start = (bf16[12288,128]{1,0:T(8,128)(2,1)S(1)}, bf16[12288,128]{1,0:T(8,128)(2,1)}, u32[]{:S(2)}) copy-start(bf16[12288,128]{1,0:T(8,128)(2,1)} %param.4) | copy-start | bytes 9437188
  11.4 7.8 %copy-start.3 = (s32[12288]{0:T(1024)S(1)}, s32[12288]{0:T(1024)}, u32[]{:S(2)}) copy-start(s32[12288]{0:T(1024)} %param.6) | copy-start | bytes 147460
  19.2 274.2 %copy-start.1 = (f32[256,128]{1,0:T(8,128)S(1)}, f32[256,128]{1,0:T(8,128)}, u32[]{:S(2)}) copy-start(f32[256,128]{1,0:T(8,128)} %param.7) | copy-start | bytes 393220
Sparse Core Ops, SparseCore 0:
  25.1 268.2 all-reduce.3
where the time goes:
time: 329 us; the launch traced here: 325 us
  waiting for transfers between devices  192 us (58%)
  blocking collectives  86.9 us (26%)
  matrix products  16.4 us (5%)
  between operations  14.1 us (4%)
  other arithmetic  8.92 us (3%)
  starting transfers between devices  4.13 us (1%)
    psum x1, waiting for transfers between devices, lloyd_update(): sums, counts = lax.psum((sums, counts), 'dp')  192 us
    psum x1, blocking collectives, lloyd_update(): sums, counts = lax.psum((sums, counts), 'dp')  69.3 us
    pmin x1, blocking collectives, on_device(): distortion = lax.pmin(local_least, 'panel')  13.8 us
    dot_general x2, matrix products, lloyd_update(): lax.dot_general(onehot, histograms, (((0,), (0,)), ((), ())), preferred_e...  13.5 us
    reduce_sum x1, other arithmetic, lloyd_update(): counts = jnp.sum(onehot, axis=0, dtype=jnp.float32)  7.04 us
  transfers between devices with their start and end apart: 2, of which 1 were waited for; matrix products, arithmetic and copies ran while one was open for 7% of the time, Pallas kernels for 0%

commit v1 on v0

v1 whole, which is shorter than its diff:
```python
import jax
import jax.numpy as jnp
from jax import lax
from jax.experimental import pallas as pl
from jax.experimental.pallas import tpu as pltpu
from jax.sharding import PartitionSpec as P

MESH = pl.DeviceIdType.MESH
F32, BF16 = jnp.float32, jnp.bfloat16
NYH, NZ, NCORE = 2, 8, 2
CHIPS = NYH * NZ
PANELS, BINS2 = 4, 2
ROWS, LANES = 12288, 128
PANEL_ROWS = 256
HALF = PANEL_ROWS // NCORE
OWN = HALF // CHIPS
PRIOR = 384.0
PART = ROWS // (PANELS * BINS2)
CHUNK = 1024
NCHUNK = ROWS // CHUNK
TILE = 256

(S_ROWS, S_PART, S_SIB, S_FWD, S_PAIR, S_SUMS, S_CENT, S_COPY, S_PANEL, S_NORM, S_LEAST, N_SEM) = range(12)


def kernel(hist, first, second, start, cent_out, dist_out,
           hv, rows, acc, pair, sib, red, sums, cent, full, norms, norm_col, least, least_all,
           load_sem, send_sem, recv_sem):
    dp, panel, half_bin = lax.axis_index("dp"), lax.axis_index("panel"), lax.axis_index("bin")
    yh, z, core = dp // (NZ * NCORE), lax.rem(dp // NCORE, NZ), lax.rem(dp, NCORE)
    chip = yh * NZ + z
    other = 1 - core
    sib_dp = chip * NCORE + other
    bin_peer = 1 - half_bin

    def device(dp_to, panel_to, bin_to):
        return {"dp": dp_to, "panel": panel_to, "bin": bin_to}

    def chip_at(shift):
        yh_to = lax.rem(yh + shift // NZ, NYH)
        return yh_to * NZ + lax.rem(z + shift % NZ, NZ)

    def panel_at(shift):
        return lax.rem(panel + shift, PANELS)

    def remote(src, dst, sem, to):
        return pltpu.make_async_remote_copy(
            src_ref=src, dst_ref=dst, send_sem=send_sem.at[sem], recv_sem=recv_sem.at[sem],
            device_id=to, device_id_type=MESH)

    def wait(ref, sem):
        pltpu.make_async_copy(ref, ref, sem).wait()

    seven = rows.at[pl.ds(0, 7 * HALF), pl.ds(0, LANES)]
    sibling = device(sib_dp, panel, half_bin)
    shifts = sorted(range(1, CHIPS), key=lambda s: -min(s % NZ, NZ - s % NZ))
    chips = [(s, chip_at(s)) for s in shifts]
    around = [(dx, db) for dx in (2, 1, 3, 0) for db in (1, 0) if dx or db]

    barrier = pltpu.get_barrier_semaphore()
    peers = [sibling]
    peers += [device(q * NCORE + core, panel, half_bin) for _, q in chips]
    peers += [device(dp, panel_at(dx), bin_peer if db else half_bin) for dx, db in around]
    peers += [device(sib_dp, panel_at(dx), half_bin) for dx in (1, 2, 3)]
    for to in peers:
        pl.semaphore_signal(barrier, inc=1, device_id=to, device_id_type=MESH)

    loads = []
    for i in range(NCHUNK):
        at = pl.ds(i * CHUNK, CHUNK)
        load = pltpu.make_async_copy(hist.at[at], hv.at[at, pl.ds(0, LANES)], load_sem.at[i])
        load.start()
    own_part = half_bin * (ROWS // 2) + panel * PART
    peer_part = bin_peer * (ROWS // 2) + panel * PART
    own_rows = pltpu.make_async_copy(
        hist.at[pl.ds(own_part, PART)], rows.at[pl.ds(0, PART), pl.ds(0, LANES)], load_sem.at[NCHUNK])
    own_rows.start()

    hv[:, LANES:] = jnp.ones((ROWS, LANES), BF16)
    acc[...] = jnp.zeros_like(acc)

    pl.semaphore_wait(barrier, len(peers))
    to_peer = remote(hist.at[pl.ds(peer_part, PART)], rows.at[pl.ds(0, PART), pl.ds(LANES, LANES)], S_PART,
                     device(dp, panel, bin_peer))
    to_sib = remote(hist.at[pl.ds(own_part, PART)], rows.at[pl.ds(PART, PART), pl.ds(0, LANES)], S_SIB, sibling)
    to_peer.start()
    to_sib.start()

    with jax.named_scope("local_sums"):
        bucket = lax.broadcasted_iota(jnp.int32, (PANEL_ROWS, LANES), 0).astype(F32).astype(BF16)
        one, zero = jnp.ones((), BF16), jnp.zeros((), BF16)

        def step(i, carry):
            at = pl.ds(pl.multiple_of(i * CHUNK, CHUNK), CHUNK)
            wait(hv.at[at, pl.ds(0, LANES)], load_sem.at[i])
            hots = []
            for assign in (first, second):
                ids = assign[pl.ds(pl.multiple_of(i * 8, 8), 8), :] - panel * PANEL_ROWS
                ids = ids.astype(F32)
                hots.append(jnp.concatenate([
                    jnp.where(jnp.broadcast_to(ids[j:j + 1, :], (PANEL_ROWS, LANES)).astype(BF16) == bucket, one, zero)
                    for j in range(CHUNK // LANES)], axis=1))
            hot = jnp.concatenate(hots, axis=0)
            acc[...] += jnp.dot(hot, hv[at, :], preferred_element_type=F32)
            return carry

        lax.fori_loop(0, NCHUNK, step, 0)

    with jax.named_scope("pair_sums"):
        lane = lax.broadcasted_iota(jnp.int32, (PANEL_ROWS, LANES), 1)
        count = jnp.where(lane < LANES // 2, acc[:PANEL_ROWS, LANES:], acc[PANEL_ROWS:, LANES:])
        groups = (PANEL_ROWS // OWN, OWN, LANES)
        pair[:, 0] = acc[:PANEL_ROWS, :LANES].reshape(groups)
        pair[:, 1] = acc[PANEL_ROWS:, :LANES].reshape(groups)
        pair[:, 2] = count.reshape(groups)
        to_pair = remote(pair.at[pl.ds(other * CHIPS, CHIPS)], sib, S_PAIR, sibling)
        to_pair.start()
        to_pair.wait_recv()
        red[...] = pair[pl.ds(core * CHIPS, CHIPS)] + sib[...]

    with jax.named_scope("chip_sums"):
        for i, (s, q) in enumerate(chips):
            remote(red.at[q], sums.at[i], S_SUMS, device(q * NCORE + core, panel, half_bin)).start()
        wait(sums, recv_sem.at[S_SUMS])
        total = red[chip]
        for i in range(CHIPS - 1):
            total += sums[i]
        here = pl.ds(pl.multiple_of(core * HALF + chip * OWN, OWN), OWN)
        middle = (total[0] + PRIOR * start[here, :]) / (total[2, :, 0:1] + PRIOR)
        cent[here, :] = (total[1] + PRIOR * middle) / (total[2, :, LANES // 2:LANES // 2 + 1] + PRIOR)

    with jax.named_scope("gather_chips"):
        for s, q in chips:
            remote(cent.at[here], cent.at[here], S_CENT, device(q * NCORE + core, panel, half_bin)).start()
        to_peer.wait_recv()
        forward = remote(rows.at[pl.ds(0, PART), pl.ds(LANES, LANES)], rows.at[pl.ds(PART, PART), pl.ds(LANES, LANES)],
                         S_FWD, sibling)
        forward.start()
        wait(cent.at[pl.ds(0, HALF - OWN)], recv_sem.at[S_CENT])

    with jax.named_scope("gather_panels"):
        mine = pl.ds(pl.multiple_of(core * HALF, HALF), HALF)
        to_copy = remote(cent.at[mine], cent.at[mine], S_COPY, sibling)
        value = cent[mine, :]
        full[pl.ds(0, HALF), pl.ds(0, LANES)] = (-2.0 * value).astype(BF16)
        for dx, db in around:
            remote(full.at[pl.ds(0, HALF), pl.ds(0, LANES)],
                   full.at[pl.ds((PANELS - dx) % PANELS * HALF, HALF), pl.ds(db * LANES, LANES)],
                   S_PANEL, device(dp, panel_at(dx), bin_peer if db else half_bin)).start()
        norms[0] = jnp.sum((value * value).T, axis=0, keepdims=True)
        for dx, db in around:
            remote(norms.at[0], norms.at[db * PANELS + (PANELS - dx) % PANELS],
                   S_NORM, device(dp, panel_at(dx), bin_peer if db else half_bin)).start()
        to_copy.start()
        own_rows.wait()
        to_sib.wait_recv()
        forward.wait_recv()
        wait(norms.at[pl.ds(1, 7)], recv_sem.at[S_NORM])
        for j in range(PANELS):
            row = norms[j] + norms[PANELS + j]
            norm_col[pl.ds(j * HALF, HALF), :] = jnp.broadcast_to(row, (HALF, HALF)).T
        wait(seven, recv_sem.at[S_PANEL])

    with jax.named_scope("least"):
        for t in range(2 * PART // TILE):
            dots = lax.dot_general(full[...], rows[pl.ds(t * TILE, TILE), :], (((1,), (1,)), ((), ())),
                                   preferred_element_type=F32)
            col = norm_col[...]
            value = dots + jnp.concatenate([col, col], axis=1)
            at = pl.ds(t * TILE % PART, TILE)
            least[t * TILE // PART, :, at] = jnp.min(value, axis=0, keepdims=True)

    with jax.named_scope("gather_least"):
        for dx in (2, 1, 3):
            remote(least.at[0], least_all.at[panel], S_LEAST, device(dp, panel_at(dx), half_bin)).start()
        for dx in (2, 1, 3, 0):
            remote(least.at[1], least_all.at[PANELS + panel], S_LEAST, device(sib_dp, panel_at(dx), half_bin)).start()
        least_all[panel] = least[0]
        to_copy.wait_recv()
        cent_out[...] = cent[...]
        wait(least_all.at[pl.ds(0, 7)], recv_sem.at[S_LEAST])
        dist_out[...] = jnp.minimum(least_all[pl.ds(0, PANELS)], least_all[pl.ds(PANELS, PANELS)])

    to_peer.wait_send()
    to_sib.wait_send()
    to_pair.wait_send()
    wait(sums, send_sem.at[S_SUMS])
    wait(cent.at[pl.ds(0, HALF - OWN)], send_sem.at[S_CENT])
    forward.wait_send()
    to_copy.wait_send()
    wait(seven, send_sem.at[S_PANEL])
    wait(norms.at[pl.ds(1, 7)], send_sem.at[S_NORM])
    wait(least_all.at[pl.ds(0, 7)], send_sem.at[S_LEAST])


def on_device(histograms, first_assign, second_assign, start_centroids):
    vmem = pl.BlockSpec(memory_space=pltpu.VMEM)
    cent, dist = pl.pallas_call(
        kernel,
        out_shape=(
            jax.ShapeDtypeStruct((PANEL_ROWS, LANES), F32),
            jax.ShapeDtypeStruct((PANELS, 1, PART), F32),
        ),
        in_specs=[pl.BlockSpec(memory_space=pltpu.HBM), vmem, vmem, vmem],
        out_specs=(vmem, vmem),
        scratch_shapes=[
            pltpu.VMEM((ROWS, 2 * LANES), BF16),
            pltpu.VMEM((2 * PART, 2 * LANES), BF16),
            pltpu.VMEM((2 * PANEL_ROWS, 2 * LANES), F32),
            pltpu.VMEM((PANEL_ROWS // OWN, 3, OWN, LANES), F32),
            pltpu.VMEM((CHIPS, 3, OWN, LANES), F32),
            pltpu.VMEM((CHIPS, 3, OWN, LANES), F32),
            pltpu.VMEM((CHIPS - 1, 3, OWN, LANES), F32),
            pltpu.VMEM((PANEL_ROWS, LANES), F32),
            pltpu.VMEM((PANELS * HALF, 2 * LANES), BF16),
            pltpu.VMEM((BINS2 * PANELS, 1, HALF), F32),
            pltpu.VMEM((PANELS * HALF, LANES), F32),
            pltpu.VMEM((2, 1, PART), F32),
            pltpu.VMEM((2 * PANELS, 1, PART), F32),
            pltpu.SemaphoreType.DMA((NCHUNK + 1,)),
            pltpu.SemaphoreType.DMA((N_SEM,)),
            pltpu.SemaphoreType.DMA((N_SEM,)),
        ],
        compiler_params=pltpu.CompilerParams(
            collective_id=0, has_side_effects=True, vmem_limit_bytes=32 * 1024 * 1024),
    )(histograms, first_assign.reshape(ROWS // LANES, LANES), second_assign.reshape(ROWS // LANES, LANES),
      start_centroids)
    return cent, dist.reshape(PANELS * PART)


def solution(mesh):
    return jax.shard_map(
        on_device,
        mesh=mesh,
        in_specs=(P("dp", "bin"), P("dp"), P("dp"), P("panel", "bin")),
        out_specs=(P("panel", "bin"), P(("dp", "bin"))),
        check_vma=False,
    )
```

time: 329 us -> 48 us (0.15); the launches traced: 325 us -> 47.8 us
  waiting for transfers between devices: 192 us -> 0 us
  blocking collectives: 86.9 us -> 0 us
  Pallas kernels: 0 us -> 41.5 us
  matrix products: 16.4 us -> 0 us
  between operations: 14.1 us -> 0.65 us
  other arithmetic: 8.92 us -> 0 us
  starting transfers between devices: 4.13 us -> 0 us
    psum x1 -> x0, waiting for transfers between devices: 192 us -> none  [lloyd_update(): sums, counts = lax.psum((sums, counts), 'dp')]
    psum x1 -> x0, blocking collectives: 69.3 us -> none  [lloyd_update(): sums, counts = lax.psum((sums, counts), 'dp')]
    pallas_call x0 -> x1, Pallas kernels: none -> 41.5 us  [on_device(): pl.pallas_call(kernel, out_shape=(jax.ShapeDtypeStruct((PANEL_ROWS, LANES...]
    dot_general x3 -> x0, matrix products: 16.4 us -> none  [the longest x2 13.5 us: lloyd_update(): lax.dot_general(onehot, histograms, (((0,), (0,)), ((), ())), preferred_e...]
    pmin x1 -> x0, blocking collectives: 13.8 us -> none  [on_device(): distortion = lax.pmin(local_least, 'panel')]
    reduce_sum x2 -> x0, other arithmetic: 7.15 us -> none  [the longest x1 7.04 us: lloyd_update(): counts = jnp.sum(onehot, axis=0, dtype=jnp.float32)]
    unnamed x8 -> x10, local copies, waits for them, and re-layouts: 0.02 us -> 5.65 us
    all_to_all x1 -> x0, starting transfers between devices: 4.09 us -> none  [on_device(): lax.all_to_all(histograms, 'bin', split_axis=0, concat_axis=1, tiled=True)]
  transfers between devices with their start and end apart: 2 -> 0, of which waited for: 1 -> 0; matrix products, arithmetic and copies ran while one was open for 7% -> 0% of each run, Pallas kernels for 0% -> 0%
where the time goes in v1:
time: 48 us; the launch traced here: 47.8 us
  Pallas kernels  41.5 us (86%)
  local copies, waits for them, and re-layouts  5.65 us (12%)
  between operations  0.65 us (1%)
    pallas_call x1, Pallas kernels, on_device(): pl.pallas_call(kernel, out_shape=(jax.ShapeDtypeStruct((PANEL_ROWS, LANES...  41.5 us
    unnamed x10, local copies, waits for them, and re-layouts  5.65 us

profile of v1, /device:TPU:1, one launch (start us, length us, event | category | flops | bytes accessed | tf_op | source)
XLA Modules:
  0.0 47.8 jit_solution(6582407573764761423)
XLA Ops:
  0.6 0.0 copy-start
  0.6 1.9 %copy-done = bf16[12288,128]{1,0:T(8,128)(2,1)S(1)} copy-done((bf16[12288,128]{1,0:T(8,128)(2,1)S(1)}, bf16[12288,128]{1,0:T(8,128)(2,1)}, u32[]{:S(2)}) %copy-start) | copy-done | bytes 3145752
  2.5 0.0 copy-start.1
  2.5 0.9 %copy-done.1 = f32[256,128]{1,0:T(8,128)S(1)} copy-done((f32[256,128]{1,0:T(8,128)S(1)}, f32[256,128]{1,0:T(8,128)}, u32[]{:S(2)}) %copy-start.1) | copy-done | bytes 131096
  3.4 0.0 copy-start.2
  3.4 0.8 %copy-done.2 = s32[12288]{0:T(1024)S(1)} copy-done((s32[12288]{0:T(1024)S(1)}, s32[12288]{0:T(1024)}, u32[]{:S(2)}) %copy-start.2) | copy-done | bytes 49176
  4.2 0.0 copy-start.3
  4.2 0.8 %copy-done.3 = s32[12288]{0:T(1024)S(1)} copy-done((s32[12288]{0:T(1024)S(1)}, s32[12288]{0:T(1024)}, u32[]{:S(2)}) %copy-start.3) | copy-done | bytes 49176
  5.0 41.5 %shard_map.59 = (f32[256,128]{1,0:T(8,128)S(1)}, f32[4,1,1536]{2,1,0:T(1,128)S(1)}) custom-call(bf16[12288,128]{1,0:T(8,128)(2,1)S(1)} %copy-done, s32[96,128]{1,0:T(8,128)S(1)} %bitcast.3, s32[96,128]{1,0:T(8,128)S(1)} %bitcast.4, f32[256,128]{1,0:T(8,128)S(1)} %copy-done.1), custom_call_target="tpu_custom_call" | custom-call | tf_op jit(solution)/shard_map/pallas_call | solution.py:198
  46.5 0.7 %copy.8 = f32[256,128]{1,0:T(8,128)} copy(f32[256,128]{1,0:T(8,128)S(1)} %get-tuple-element.8) | data formatting | bytes 262144
  47.2 0.6 %copy.9 = f32[6144]{0:T(1024)} copy(f32[6144]{0:T(1024)S(1)} %bitcast.5) | data formatting | bytes 49152
Async XLA Ops:
  0.6 1.9 %copy-start = (bf16[12288,128]{1,0:T(8,128)(2,1)S(1)}, bf16[12288,128]{1,0:T(8,128)(2,1)}, u32[]{:S(2)}) copy-start(bf16[12288,128]{1,0:T(8,128)(2,1)} %hist.1) | copy-start | bytes 9437188
  2.5 0.9 %copy-start.1 = (f32[256,128]{1,0:T(8,128)S(1)}, f32[256,128]{1,0:T(8,128)}, u32[]{:S(2)}) copy-start(f32[256,128]{1,0:T(8,128)} %start.1) | copy-start | bytes 393220
  3.4 0.8 %copy-start.2 = (s32[12288]{0:T(1024)S(1)}, s32[12288]{0:T(1024)}, u32[]{:S(2)}) copy-start(s32[12288]{0:T(1024)} %param.5) | copy-start | bytes 147460
  4.2 0.8 %copy-start.3 = (s32[12288]{0:T(1024)S(1)}, s32[12288]{0:T(1024)}, u32[]{:S(2)}) copy-start(s32[12288]{0:T(1024)} %param.6) | copy-start | bytes 147460

commit v2 on v0

v2 whole, which is shorter than its diff:
```python
import jax
import jax.numpy as jnp
from jax import lax
from jax.experimental import pallas as pl
from jax.experimental.pallas import tpu as pltpu
from jax.sharding import PartitionSpec as P

MESH = pl.DeviceIdType.MESH
F32, BF16 = jnp.float32, jnp.bfloat16
NYH, NZ, NCORE = 2, 8, 2
CHIPS = NYH * NZ
PANELS = 4
ROWS, LANES = 12288, 128
OUT_ROWS = ROWS // 2
PANEL_ROWS = 256
HALF = PANEL_ROWS // NCORE
OWN = HALF // CHIPS
PRIOR = 384.0
CHUNKS = (2048, 4096, 6144)
TILE = 256
DIRECT = 1536
QUARTER = (OUT_ROWS - DIRECT) // PANELS
PIECES = 3
PIECE = QUARTER // PIECES

(S_DIRECT, S_ACROSS, S_PAIR, S_SUMS, S_COUNTS, S_CENT, S_COPY, S_LEAST, S_PIECE) = range(9)
N_SEM = S_PIECE + PIECES


def kernel(hist, first_in, second_in, start_in, cent_out, dist_out,
           hv, first, second, start, rows, acc, pair, sib, red, sums, count, counts, cent, full, norm, least,
           load_sem, send_sem, recv_sem):
    dp, panel, half_bin = lax.axis_index("dp"), lax.axis_index("panel"), lax.axis_index("bin")
    yh, z, core = dp // (NZ * NCORE), lax.rem(dp // NCORE, NZ), lax.rem(dp, NCORE)
    chip = yh * NZ + z
    other = 1 - core
    bin_peer = 1 - half_bin

    def device(dp_to, panel_to, bin_to):
        return {"dp": dp_to, "panel": panel_to, "bin": bin_to}

    def chip_at(shift):
        yh_to = lax.rem(yh + shift // NZ, NYH)
        return yh_to * NZ + lax.rem(z + shift % NZ, NZ)

    def remote(src, dst, sem, to):
        return pltpu.make_async_remote_copy(
            src_ref=src, dst_ref=dst, send_sem=send_sem.at[sem], recv_sem=recv_sem.at[sem],
            device_id=to, device_id_type=MESH)

    def wait(ref, sem):
        pltpu.make_async_copy(ref, ref, sem).wait()

    sibling = device(chip * NCORE + other, panel, half_bin)
    across = [device(dp, lax.rem(panel + dx, PANELS), half_bin) for dx in (2, 1, 3)]
    shifts = sorted(range(CHIPS), key=lambda s: -min(s % NZ, NZ - s % NZ) - 2 * (s // NZ))
    chips = [chip_at(s) for s in shifts if s]
    same_bin = [device(q * NCORE + core, panel, half_bin) for q in chips]
    other_bin = [device(chip_at(s) * NCORE + core, panel, bin_peer) for s in shifts]

    barrier = pltpu.get_barrier_semaphore()
    peers = same_bin + other_bin + across + [sibling]
    for to in peers:
        pl.semaphore_signal(barrier, inc=1, device_id=to, device_id_type=MESH)

    small = [pltpu.make_async_copy(src, dst, load_sem.at[i])
             for i, (src, dst) in enumerate(((first_in, first), (second_in, second), (start_in, start)))]
    begins = [sum(CHUNKS[:i]) for i in range(len(CHUNKS))]
    loads = [pltpu.make_async_copy(hist.at[pl.ds(at, n)], hv.at[pl.ds(at, n), pl.ds(0, LANES)], load_sem.at[3 + i])
             for i, (at, n) in enumerate(zip(begins, CHUNKS))]
    own_rows = pltpu.make_async_copy(
        hist.at[pl.ds(half_bin * OUT_ROWS, OUT_ROWS)], rows.at[:, pl.ds(0, LANES)], load_sem.at[3 + len(CHUNKS)])
    for copy in small[:2] + loads + small[2:] + [own_rows]:
        copy.start()

    hv[:, LANES:] = jnp.ones((ROWS, LANES), BF16)

    with jax.named_scope("local_sums"):
        bucket = lax.broadcasted_iota(jnp.int32, (PANEL_ROWS, LANES), 0).astype(F32).astype(BF16)
        one, zero = jnp.ones((), BF16), jnp.zeros((), BF16)
        for copy in small[:2]:
            copy.wait()
        for at, n, load in zip(begins, CHUNKS, loads):
            hots = []
            for assign in (first, second):
                ids = (assign[at // LANES:(at + n) // LANES, :] - panel * PANEL_ROWS).astype(F32)
                hots.append(jnp.concatenate([
                    jnp.where(jnp.broadcast_to(ids[j:j + 1, :], (PANEL_ROWS, LANES)).astype(BF16) == bucket, one, zero)
                    for j in range(n // LANES)], axis=1))
            hot = jnp.concatenate(hots, axis=0)
            load.wait()
            part = jnp.dot(hot, hv[at:at + n, :], preferred_element_type=F32)
            if at:
                acc[...] += part
            else:
                acc[...] = part

    pl.semaphore_wait(barrier, len(peers))

    with jax.named_scope("pair_sums"):
        lane = lax.broadcasted_iota(jnp.int32, (PANEL_ROWS, LANES), 1)
        both = jnp.where(lane < LANES // 2, acc[:PANEL_ROWS, LANES:], acc[PANEL_ROWS:, LANES:])
        groups = (PANEL_ROWS // OWN, OWN, LANES)
        pair[:, 0] = acc[:PANEL_ROWS, :LANES].reshape(groups)
        pair[:, 1] = acc[PANEL_ROWS:, :LANES].reshape(groups)
        pair[:, 2] = both.reshape(groups)
        to_pair = remote(pair.at[pl.ds(other * CHIPS, CHIPS)], sib, S_PAIR, sibling)
        to_pair.start()

        base = bin_peer * OUT_ROWS
        peer = device(dp, panel, bin_peer)
        quarter = DIRECT + panel * QUARTER
        pieces = [remote(hist.at[pl.ds(base + quarter + i * PIECE, PIECE)],
                         rows.at[pl.ds(quarter + i * PIECE, PIECE), pl.ds(LANES, LANES)], S_PIECE + i, peer)
                  for i in range(PIECES)]
        direct = remote(hist.at[pl.ds(base, DIRECT)], rows.at[pl.ds(0, DIRECT), pl.ds(LANES, LANES)], S_DIRECT, peer)
        for copy in pieces + [direct]:
            copy.start()

        to_pair.wait_recv()
        own = pl.ds(core * CHIPS, CHIPS)
        red[...] = pair[own, 0:2] + sib[:, 0:2]
        turned = (pair[own, 2] + sib[:, 2]).reshape(HALF, LANES).T
        count[0] = turned[0:1, :]
        count[1] = turned[LANES // 2:LANES // 2 + 1, :]

    with jax.named_scope("chip_sums"):
        for i, (q, to) in enumerate(zip(chips, same_bin)):
            remote(red.at[q], sums.at[i], S_SUMS, to).start()
            remote(count, counts.at[i], S_COUNTS, to).start()
        for i, copy in enumerate(pieces):
            copy.wait_recv()
            at = rows.at[pl.ds(quarter + i * PIECE, PIECE), pl.ds(LANES, LANES)]
            for to in across:
                remote(at, at, S_ACROSS, to).start()
        for copy in small[2:]:
            copy.wait()
        wait(counts, recv_sem.at[S_COUNTS])
        number = count[...]
        for i in range(CHIPS - 1):
            number += counts[i]
        mark = (lax.broadcasted_iota(jnp.int32, (OWN, LANES), 1)
                == lax.broadcasted_iota(jnp.int32, (OWN, LANES), 0) + chip * OWN)
        weight = [jnp.sum(jnp.where(mark, jnp.broadcast_to(number[s], (OWN, LANES)), 0.0), axis=1, keepdims=True) + PRIOR
                  for s in range(2)]
        here = pl.ds(pl.multiple_of(core * HALF + chip * OWN, OWN), OWN)
        before = PRIOR * start[here, :]
        wait(sums, recv_sem.at[S_SUMS])
        total = red[chip]
        for i in range(CHIPS - 1):
            total += sums[i]
        middle = (total[0] + before) / weight[0]
        cent[0, here, :] = (total[1] + PRIOR * middle) / weight[1]

    with jax.named_scope("gather_chips"):
        for i in range(CHIPS):
            remote(cent.at[0, here], cent.at[1, here], S_CENT, other_bin[i]).start()
            if i < CHIPS - 1:
                remote(cent.at[0, here], cent.at[0, here], S_CENT, same_bin[i]).start()
        slices = acc.at[pl.ds(0, 2 * HALF - OWN), pl.ds(0, LANES)]
        wait(slices, recv_sem.at[S_CENT])

    with jax.named_scope("gather_cores"):
        mine = pl.ds(pl.multiple_of(core * HALF, HALF), HALF)
        theirs = pl.ds(pl.multiple_of(other * HALF, HALF), HALF)
        to_copy = remote(cent.at[:, mine], cent.at[:, mine], S_COPY, sibling)
        to_copy.start()

        def prepare(at, buckets):
            value = jnp.concatenate([cent[0, at, :], cent[1, at, :]], axis=1)
            full[buckets, :] = (-2.0 * value).astype(BF16)
            norm[buckets, :] = jnp.broadcast_to(jnp.sum(value * value, axis=1, keepdims=True), (HALF, LANES))

        prepare(mine, slice(0, HALF))
        own_rows.wait()
        to_copy.wait_recv()
        prepare(theirs, slice(HALF, PANEL_ROWS))
        direct.wait_recv()
        wait(rows.at[pl.ds(0, (PANELS - 1) * QUARTER), pl.ds(LANES, LANES)], recv_sem.at[S_ACROSS])

    with jax.named_scope("least"):
        for t in range(OUT_ROWS // TILE):
            dots = lax.dot_general(full[...], rows[t * TILE:(t + 1) * TILE, :], (((1,), (1,)), ((), ())),
                                   preferred_element_type=F32)
            value = dots + jnp.concatenate([norm[...]] * (TILE // LANES), axis=1)
            least[0, :, t * TILE:(t + 1) * TILE] = jnp.min(value, axis=0, keepdims=True)
            if (t + 1) * TILE in (OUT_ROWS // 2, OUT_ROWS):
                part = pl.ds((t + 1) * TILE - OUT_ROWS // 2, OUT_ROWS // 2)
                for dx, to in zip((2, 1, 3), across):
                    remote(least.at[0, :, part], least.at[dx, :, part], S_LEAST, to).start()
        cent_out[...] = cent[0]
        wait(least.at[pl.ds(1, PANELS - 1)], recv_sem.at[S_LEAST])
        dist_out[...] = jnp.minimum(jnp.minimum(least[0], least[1]), jnp.minimum(least[2], least[3]))

    to_pair.wait_send()
    for copy in pieces + [direct]:
        copy.wait_send()
    wait(sums, send_sem.at[S_SUMS])
    wait(counts, send_sem.at[S_COUNTS])
    wait(rows.at[pl.ds(0, (PANELS - 1) * QUARTER), pl.ds(LANES, LANES)], send_sem.at[S_ACROSS])
    wait(slices, send_sem.at[S_CENT])
    to_copy.wait_send()
    wait(least.at[pl.ds(1, PANELS - 1)], send_sem.at[S_LEAST])


def on_device(histograms, first_assign, second_assign, start_centroids):
    vmem = pl.BlockSpec(memory_space=pltpu.VMEM)
    args = [pltpu.with_memory_space_constraint(a, pltpu.HBM) for a in (
        histograms, first_assign.reshape(ROWS // LANES, LANES), second_assign.reshape(ROWS // LANES, LANES),
        start_centroids)]
    cent, dist = pl.pallas_call(
        kernel,
        out_shape=(pltpu.VMEM((PANEL_ROWS, LANES), F32), pltpu.VMEM((1, OUT_ROWS), F32)),
        in_specs=[pl.BlockSpec(memory_space=pltpu.HBM)] * 4,
        out_specs=(vmem, vmem),
        scratch_shapes=[
            pltpu.VMEM((ROWS, 2 * LANES), BF16),
            pltpu.VMEM((ROWS // LANES, LANES), jnp.int32),
            pltpu.VMEM((ROWS // LANES, LANES), jnp.int32),
            pltpu.VMEM((PANEL_ROWS, LANES), F32),
            pltpu.VMEM((OUT_ROWS, 2 * LANES), BF16),
            pltpu.VMEM((2 * PANEL_ROWS, 2 * LANES), F32),
            pltpu.VMEM((PANEL_ROWS // OWN, 3, OWN, LANES), F32),
            pltpu.VMEM((CHIPS, 3, OWN, LANES), F32),
            pltpu.VMEM((CHIPS, 2, OWN, LANES), F32),
            pltpu.VMEM((CHIPS - 1, 2, OWN, LANES), F32),
            pltpu.VMEM((2, 1, LANES), F32),
            pltpu.VMEM((CHIPS - 1, 2, 1, LANES), F32),
            pltpu.VMEM((2, PANEL_ROWS, LANES), F32),
            pltpu.VMEM((PANEL_ROWS, 2 * LANES), BF16),
            pltpu.VMEM((PANEL_ROWS, LANES), F32),
            pltpu.VMEM((PANELS, 1, OUT_ROWS), F32),
            pltpu.SemaphoreType.DMA((len(CHUNKS) + 4,)),
            pltpu.SemaphoreType.DMA((N_SEM,)),
            pltpu.SemaphoreType.DMA((N_SEM,)),
        ],
        compiler_params=pltpu.CompilerParams(
            collective_id=0, has_side_effects=True, vmem_limit_bytes=48 * 1024 * 1024),
    )(*args)
    return cent, dist.reshape(OUT_ROWS)


def solution(mesh):
    return jax.shard_map(
        on_device,
        mesh=mesh,
        in_specs=(P("dp", "bin"), P("dp"), P("dp"), P("panel", "bin")),
        out_specs=(P("panel", "bin"), P(("dp", "bin"))),
        check_vma=False,
    )
```

time: 329 us -> 48.3 us (0.15); the launches traced: 325 us -> 48.2 us
  waiting for transfers between devices: 192 us -> 0 us
  blocking collectives: 86.9 us -> 0 us
  Pallas kernels: 0 us -> 46.3 us
  matrix products: 16.4 us -> 0 us
  between operations: 14.1 us -> 0.64 us
  other arithmetic: 8.92 us -> 0 us
  starting transfers between devices: 4.13 us -> 0 us
    psum x1 -> x0, waiting for transfers between devices: 192 us -> none  [lloyd_update(): sums, counts = lax.psum((sums, counts), 'dp')]
    psum x1 -> x0, blocking collectives: 69.3 us -> none  [lloyd_update(): sums, counts = lax.psum((sums, counts), 'dp')]
    pallas_call x0 -> x1, Pallas kernels: none -> 46.3 us  [on_device(): pl.pallas_call(kernel, out_shape=(pltpu.VMEM((PANEL_ROWS, LANES), F32), p...]
    dot_general x3 -> x0, matrix products: 16.4 us -> none  [the longest x2 13.5 us: lloyd_update(): lax.dot_general(onehot, histograms, (((0,), (0,)), ((), ())), preferred_e...]
    pmin x1 -> x0, blocking collectives: 13.8 us -> none  [on_device(): distortion = lax.pmin(local_least, 'panel')]
    reduce_sum x2 -> x0, other arithmetic: 7.15 us -> none  [the longest x1 7.04 us: lloyd_update(): counts = jnp.sum(onehot, axis=0, dtype=jnp.float32)]
    all_to_all x1 -> x0, starting transfers between devices: 4.09 us -> none  [on_device(): lax.all_to_all(histograms, 'bin', split_axis=0, concat_axis=1, tiled=True)]
    all_gather x1 -> x0, blocking collectives: 3.8 us -> none  [on_device(): lax.all_gather(centroids.astype(jnp.bfloat16), 'bin', axis=1, tiled=True)]
  transfers between devices with their start and end apart: 2 -> 0, of which waited for: 1 -> 0; matrix products, arithmetic and copies ran while one was open for 7% -> 0% of each run, Pallas kernels for 0% -> 0%
where the time goes in v2:
time: 48.3 us; the launch traced here: 48.2 us
  Pallas kernels  46.3 us (96%)
  local copies, waits for them, and re-layouts  1.27 us (3%)
  between operations  0.64 us (1%)
    pallas_call x1, Pallas kernels, on_device(): pl.pallas_call(kernel, out_shape=(pltpu.VMEM((PANEL_ROWS, LANES), F32), p...  46.3 us
    unnamed x2, local copies, waits for them, and re-layouts  1.27 us

profile of v2, /device:TPU:1, one launch (start us, length us, event | category | flops | bytes accessed | tf_op | source)
XLA Modules:
  0.0 48.2 jit_solution(9250864131451477136)
XLA Ops:
  0.6 46.3 %shard_map.59 = (f32[256,128]{1,0:T(8,128)S(1)}, f32[1,6144]{1,0:T(1,128)S(1)}) custom-call(bf16[12288,128]{1,0:T(8,128)(2,1)} %hist.1, s32[96,128]{1,0:T(8,128)} %bitcast.4, s32[96,128]{1,0:T(8,128)} %bitcast.5, f32[256,128]{1,0:T(8,128)} %start_in.1), custom_call_target="tpu_custom_call" | custom-call | tf_op jit(solution)/shard_map/pallas_call | solution.py:211
  47.0 0.7 %copy.8 = f32[256,128]{1,0:T(8,128)} copy(f32[256,128]{1,0:T(8,128)S(1)} %get-tuple-element.6) | data formatting | bytes 262144
  47.6 0.6 %copy.9 = f32[6144]{0:T(1024)} copy(f32[6144]{0:T(1024)S(1)} %bitcast.3) | data formatting | bytes 49152

commit v3 on v2

--- a/solution.py
+++ b/solution.py
@@ -18,18 +18,18 @@
 PRIOR = 384.0
 CHUNKS = (2048, 4096, 6144)
 TILE = 256
-DIRECT = 1536
-QUARTER = (OUT_ROWS - DIRECT) // PANELS
-PIECES = 3
+QUARTER = OUT_ROWS // PANELS
+PIECES = 4
+EARLY = 4
 PIECE = QUARTER // PIECES
 
-(S_DIRECT, S_ACROSS, S_PAIR, S_SUMS, S_COUNTS, S_CENT, S_COPY, S_LEAST, S_PIECE) = range(9)
+(S_ACROSS, S_PAIR, S_SUMS, S_COUNTS, S_CENT, S_COPY, S_LEAST, S_PIECE) = range(8)
 N_SEM = S_PIECE + PIECES
 
 
 def kernel(hist, first_in, second_in, start_in, cent_out, dist_out,
            hv, first, second, start, rows, acc, pair, sib, red, sums, count, counts, cent, full, norm, least,
-           load_sem, send_sem, recv_sem):
+           load_sem, send_sem, recv_sem, near_sem, far_sem):
     dp, panel, half_bin = lax.axis_index("dp"), lax.axis_index("panel"), lax.axis_index("bin")
     yh, z, core = dp // (NZ * NCORE), lax.rem(dp // NCORE, NZ), lax.rem(dp, NCORE)
     chip = yh * NZ + z
@@ -59,9 +59,56 @@
     other_bin = [device(chip_at(s) * NCORE + core, panel, bin_peer) for s in shifts]
 
     barrier = pltpu.get_barrier_semaphore()
-    peers = same_bin + other_bin + across + [sibling]
-    for to in peers:
-        pl.semaphore_signal(barrier, inc=1, device_id=to, device_id_type=MESH)
+    near = [other_bin[-1]] + across
+    far = same_bin + other_bin[:-1]
+
+    def signal(semaphore, to):
+        pl.semaphore_signal(semaphore, inc=1, device_id=to, device_id_type=MESH)
+
+    for to in near:
+        signal(barrier, device(chip * NCORE, to["panel"], to["bin"]))
+    signal(barrier, sibling)
+    for to in far:
+        signal(barrier, device(to["dp"] - core + 1, to["panel"], to["bin"]))
+
+    def wait_near():
+        @pl.when(core == 0)
+        def _():
+            pl.semaphore_wait(barrier, NCORE * len(near) + 1)
+            signal(near_sem, sibling)
+
+        @pl.when(core == 1)
+        def _():
+            pl.semaphore_wait(near_sem, 1)
+
+    def wait_far():
+        @pl.when(core == 1)
+        def _():
+            pl.semaphore_wait(barrier, NCORE * len(far) + 1)
+            signal(far_sem, sibling)
+
+        @pl.when(core == 0)
+        def _():
+            pl.semaphore_wait(far_sem, 1)
+
+    base = bin_peer * OUT_ROWS
+    quarter = panel * QUARTER
+    pieces = [remote(hist.at[pl.ds(base + quarter + i * PIECE, PIECE)],
+                     rows.at[pl.ds(quarter + i * PIECE, PIECE), pl.ds(LANES, LANES)], S_PIECE + i, other_bin[-1])
+              for i in range(PIECES)]
+
+    def send_pieces():
+        for copy in pieces:
+            copy.start()
+
+    def pass_on(which):
+        for i in which:
+            pieces[i].wait_recv()
+            at = rows.at[pl.ds(quarter + i * PIECE, PIECE), pl.ds(LANES, LANES)]
+            for to in across:
+                remote(at, at, S_ACROSS, to).start()
+
+    early = z < EARLY
 
     small = [pltpu.make_async_copy(src, dst, load_sem.at[i])
              for i, (src, dst) in enumerate(((first_in, first), (second_in, second), (start_in, start)))]
@@ -74,6 +121,11 @@
         copy.start()
 
     hv[:, LANES:] = jnp.ones((ROWS, LANES), BF16)
+
+    @pl.when(early)
+    def _():
+        wait_near()
+        send_pieces()
 
     with jax.named_scope("local_sums"):
         bucket = lax.broadcasted_iota(jnp.int32, (PANEL_ROWS, LANES), 0).astype(F32).astype(BF16)
@@ -95,7 +147,15 @@
             else:
                 acc[...] = part
 
-    pl.semaphore_wait(barrier, len(peers))
+    @pl.when(early)
+    def _():
+        pass_on(range(PIECES))
+
+    @pl.when(jnp.logical_not(early))
+    def _():
+        wait_near()
+
+    wait_far()
 
     with jax.named_scope("pair_sums"):
         lane = lax.broadcasted_iota(jnp.int32, (PANEL_ROWS, LANES), 1)
@@ -107,16 +167,6 @@
         to_pair = remote(pair.at[pl.ds(other * CHIPS, CHIPS)], sib, S_PAIR, sibling)
         to_pair.start()
 
-        base = bin_peer * OUT_ROWS
-        peer = device(dp, panel, bin_peer)
-        quarter = DIRECT + panel * QUARTER
-        pieces = [remote(hist.at[pl.ds(base + quarter + i * PIECE, PIECE)],
-                         rows.at[pl.ds(quarter + i * PIECE, PIECE), pl.ds(LANES, LANES)], S_PIECE + i, peer)
-                  for i in range(PIECES)]
-        direct = remote(hist.at[pl.ds(base, DIRECT)], rows.at[pl.ds(0, DIRECT), pl.ds(LANES, LANES)], S_DIRECT, peer)
-        for copy in pieces + [direct]:
-            copy.start()
-
         to_pair.wait_recv()
         own = pl.ds(core * CHIPS, CHIPS)
         red[...] = pair[own, 0:2] + sib[:, 0:2]
@@ -128,11 +178,12 @@
         for i, (q, to) in enumerate(zip(chips, same_bin)):
             remote(red.at[q], sums.at[i], S_SUMS, to).start()
             remote(count, counts.at[i], S_COUNTS, to).start()
-        for i, copy in enumerate(pieces):
-            copy.wait_recv()
-            at = rows.at[pl.ds(quarter + i * PIECE, PIECE), pl.ds(LANES, LANES)]
-            for to in across:
-                remote(at, at, S_ACROSS, to).start()
+
+        @pl.when(jnp.logical_not(early))
+        def _():
+            send_pieces()
+            pass_on(range(PIECES // 2))
+
         for copy in small[2:]:
             copy.wait()
         wait(counts, recv_sem.at[S_COUNTS])
@@ -157,6 +208,11 @@
             remote(cent.at[0, here], cent.at[1, here], S_CENT, other_bin[i]).start()
             if i < CHIPS - 1:
                 remote(cent.at[0, here], cent.at[0, here], S_CENT, same_bin[i]).start()
+
+        @pl.when(jnp.logical_not(early))
+        def _():
+            pass_on(range(PIECES // 2, PIECES))
+
         slices = acc.at[pl.ds(0, 2 * HALF - OWN), pl.ds(0, LANES)]
         wait(slices, recv_sem.at[S_CENT])
 
@@ -175,7 +231,6 @@
         own_rows.wait()
         to_copy.wait_recv()
         prepare(theirs, slice(HALF, PANEL_ROWS))
-        direct.wait_recv()
         wait(rows.at[pl.ds(0, (PANELS - 1) * QUARTER), pl.ds(LANES, LANES)], recv_sem.at[S_ACROSS])
 
     with jax.named_scope("least"):
@@ -193,7 +248,7 @@
         dist_out[...] = jnp.minimum(jnp.minimum(least[0], least[1]), jnp.minimum(least[2], least[3]))
 
     to_pair.wait_send()
-    for copy in pieces + [direct]:
+    for copy in pieces:
         copy.wait_send()
     wait(sums, send_sem.at[S_SUMS])
     wait(counts, send_sem.at[S_COUNTS])
@@ -233,6 +288,8 @@
             pltpu.SemaphoreType.DMA((len(CHUNKS) + 4,)),
             pltpu.SemaphoreType.DMA((N_SEM,)),
             pltpu.SemaphoreType.DMA((N_SEM,)),
+            pltpu.SemaphoreType.REGULAR,
+            pltpu.SemaphoreType.REGULAR,
         ],
         compiler_params=pltpu.CompilerParams(
             collective_id=0, has_side_effects=True, vmem_limit_bytes=48 * 1024 * 1024),

time: 48.3 us -> 43.7 us (0.905)
  the two profiles are of different devices: /device:TPU:1 before, /device:TPU:128 now
where the time goes in v3:
time: 43.7 us; the launch traced here: 43.6 us
  Pallas kernels  41.7 us (95%)
  local copies, waits for them, and re-layouts  1.27 us (3%)
  between operations  0.64 us (1%)
    pallas_call x1, Pallas kernels, on_device(): pl.pallas_call(kernel, out_shape=(pltpu.VMEM((PANEL_ROWS, LANES), F32), p...  41.7 us
    unnamed x2, local copies, waits for them, and re-layouts  1.27 us

profile of v3, /device:TPU:128, one launch (start us, length us, event | category | flops | bytes accessed | tf_op | source)
XLA Modules:
  0.0 43.6 jit_solution(3911005462472367010)
XLA Ops:
  0.6 41.7 %shard_map.59 = (f32[256,128]{1,0:T(8,128)S(1)}, f32[1,6144]{1,0:T(1,128)S(1)}) custom-call(bf16[12288,128]{1,0:T(8,128)(2,1)} %hist.1, s32[96,128]{1,0:T(8,128)} %bitcast.4, s32[96,128]{1,0:T(8,128)} %bitcast.5, f32[256,128]{1,0:T(8,128)} %start_in.1), custom_call_target="tpu_custom_call" | custom-call | tf_op jit(solution)/shard_map/pallas_call | solution.py:266
  42.3 0.7 %copy.8 = f32[256,128]{1,0:T(8,128)} copy(f32[256,128]{1,0:T(8,128)S(1)} %get-tuple-element.6) | data formatting | bytes 262144
  43.0 0.6 %copy.9 = f32[6144]{0:T(1024)} copy(f32[6144]{0:T(1024)S(1)} %bitcast.3) | data formatting | bytes 49152

commit v4 on v3

--- a/solution.py
+++ b/solution.py
@@ -16,19 +16,19 @@
 HALF = PANEL_ROWS // NCORE
 OWN = HALF // CHIPS
 PRIOR = 384.0
-CHUNKS = (2048, 4096, 6144)
+CHUNKS = (2048, 6144, 4096)
 TILE = 256
 QUARTER = OUT_ROWS // PANELS
 PIECES = 4
-EARLY = 4
+SOON, MID = 2, 4
 PIECE = QUARTER // PIECES
 
-(S_ACROSS, S_PAIR, S_SUMS, S_COUNTS, S_CENT, S_COPY, S_LEAST, S_PIECE) = range(8)
+S_PAIR, S_SUMS, S_ACROSS, S_COUNTS, S_CENT, S_COPY, S_LEAST, S_PIECE = 0, 2, 4, 5, 6, 7, 8, 9
 N_SEM = S_PIECE + PIECES
 
 
 def kernel(hist, first_in, second_in, start_in, cent_out, dist_out,
-           hv, first, second, start, rows, acc, pair, sib, red, sums, count, counts, cent, full, norm, least,
+           hv, first, second, start, rows, acc, sib, red, sums, count, counts, cent, full, norm, least,
            load_sem, send_sem, recv_sem, near_sem, far_sem):
     dp, panel, half_bin = lax.axis_index("dp"), lax.axis_index("panel"), lax.axis_index("bin")
     yh, z, core = dp // (NZ * NCORE), lax.rem(dp // NCORE, NZ), lax.rem(dp, NCORE)
@@ -57,58 +57,6 @@
     chips = [chip_at(s) for s in shifts if s]
     same_bin = [device(q * NCORE + core, panel, half_bin) for q in chips]
     other_bin = [device(chip_at(s) * NCORE + core, panel, bin_peer) for s in shifts]
-
-    barrier = pltpu.get_barrier_semaphore()
-    near = [other_bin[-1]] + across
-    far = same_bin + other_bin[:-1]
-
-    def signal(semaphore, to):
-        pl.semaphore_signal(semaphore, inc=1, device_id=to, device_id_type=MESH)
-
-    for to in near:
-        signal(barrier, device(chip * NCORE, to["panel"], to["bin"]))
-    signal(barrier, sibling)
-    for to in far:
-        signal(barrier, device(to["dp"] - core + 1, to["panel"], to["bin"]))
-
-    def wait_near():
-        @pl.when(core == 0)
-        def _():
-            pl.semaphore_wait(barrier, NCORE * len(near) + 1)
-            signal(near_sem, sibling)
-
-        @pl.when(core == 1)
-        def _():
-            pl.semaphore_wait(near_sem, 1)
-
-    def wait_far():
-        @pl.when(core == 1)
-        def _():
-            pl.semaphore_wait(barrier, NCORE * len(far) + 1)
-            signal(far_sem, sibling)
-
-        @pl.when(core == 0)
-        def _():
-            pl.semaphore_wait(far_sem, 1)
-
-    base = bin_peer * OUT_ROWS
-    quarter = panel * QUARTER
-    pieces = [remote(hist.at[pl.ds(base + quarter + i * PIECE, PIECE)],
-                     rows.at[pl.ds(quarter + i * PIECE, PIECE), pl.ds(LANES, LANES)], S_PIECE + i, other_bin[-1])
-              for i in range(PIECES)]
-
-    def send_pieces():
-        for copy in pieces:
-            copy.start()
-
-    def pass_on(which):
-        for i in which:
-            pieces[i].wait_recv()
-            at = rows.at[pl.ds(quarter + i * PIECE, PIECE), pl.ds(LANES, LANES)]
-            for to in across:
-                remote(at, at, S_ACROSS, to).start()
-
-    early = z < EARLY
 
     small = [pltpu.make_async_copy(src, dst, load_sem.at[i])
              for i, (src, dst) in enumerate(((first_in, first), (second_in, second), (start_in, start)))]
@@ -120,12 +68,69 @@
     for copy in small[:2] + loads + small[2:] + [own_rows]:
         copy.start()
 
+    barrier = pltpu.get_barrier_semaphore()
+    near = [other_bin[-1]] + across
+    far = same_bin + other_bin[:-1]
+
+    def signal(semaphore, to):
+        pl.semaphore_signal(semaphore, inc=1, device_id=to, device_id_type=MESH)
+
+    for to in near:
+        signal(barrier, device(chip * NCORE, to["panel"], to["bin"]))
+    signal(barrier, sibling)
+    for to in far:
+        signal(barrier, device(to["dp"] - core + 1, to["panel"], to["bin"]))
+
+    def wait_near():
+        @pl.when(core == 0)
+        def _():
+            pl.semaphore_wait(barrier, NCORE * len(near) + 1)
+            signal(near_sem, sibling)
+
+        @pl.when(core == 1)
+        def _():
+            pl.semaphore_wait(near_sem, 1)
+
+    def wait_far():
+        @pl.when(core == 1)
+        def _():
+            pl.semaphore_wait(barrier, NCORE * len(far) + 1)
+            signal(far_sem, sibling)
+
+        @pl.when(core == 0)
+        def _():
+            pl.semaphore_wait(far_sem, 1)
+
+    to_pair = [remote(acc.at[s, pl.ds(pl.multiple_of(other * HALF, HALF), HALF)], sib.at[s], S_PAIR + s, sibling)
+               for s in range(2)]
+
+    base = bin_peer * OUT_ROWS
+    quarter = panel * QUARTER
+    pieces = [remote(hist.at[pl.ds(base + quarter + i * PIECE, PIECE)],
+                     rows.at[pl.ds(quarter + i * PIECE, PIECE), pl.ds(LANES, LANES)], S_PIECE + i, other_bin[-1])
+              for i in range(PIECES)]
+
+    def send_pieces(which):
+        for i in which:
+            pieces[i].start()
+
+    def pass_on(which):
+        for i in which:
+            pieces[i].wait_recv()
+            at = rows.at[pl.ds(quarter + i * PIECE, PIECE), pl.ds(LANES, LANES)]
+            for to in across:
+                remote(at, at, S_ACROSS, to).start()
+
+    soon, late = z < SOON, z >= MID
+    between = jnp.logical_and(z >= SOON, z < MID)
+    half_of = range(PIECES // 2), range(PIECES // 2, PIECES)
+
     hv[:, LANES:] = jnp.ones((ROWS, LANES), BF16)
 
-    @pl.when(early)
+    @pl.when(jnp.logical_not(late))
     def _():
         wait_near()
-        send_pieces()
+        send_pieces(range(PIECES))
 
     with jax.named_scope("local_sums"):
         bucket = lax.broadcasted_iota(jnp.int32, (PANEL_ROWS, LANES), 0).astype(F32).astype(BF16)
@@ -133,56 +138,54 @@
         for copy in small[:2]:
             copy.wait()
         for at, n, load in zip(begins, CHUNKS, loads):
-            hots = []
-            for assign in (first, second):
+            for s, assign in enumerate((first, second)):
                 ids = (assign[at // LANES:(at + n) // LANES, :] - panel * PANEL_ROWS).astype(F32)
-                hots.append(jnp.concatenate([
+                hot = jnp.concatenate([
                     jnp.where(jnp.broadcast_to(ids[j:j + 1, :], (PANEL_ROWS, LANES)).astype(BF16) == bucket, one, zero)
-                    for j in range(n // LANES)], axis=1))
-            hot = jnp.concatenate(hots, axis=0)
-            load.wait()
-            part = jnp.dot(hot, hv[at:at + n, :], preferred_element_type=F32)
-            if at:
-                acc[...] += part
-            else:
-                acc[...] = part
-
-    @pl.when(early)
+                    for j in range(n // LANES)], axis=1)
+                if s == 0:
+                    load.wait()
+                part = jnp.dot(hot, hv[at:at + n, :], preferred_element_type=F32)
+                acc[s] = acc[s] + part if at else part
+                if at == begins[-1]:
+                    to_pair[s].start()
+            if at == begins[0]:
+                @pl.when(late)
+                def _():
+                    wait_near()
+                    send_pieces(half_of[0])
+
+    @pl.when(soon)
     def _():
         pass_on(range(PIECES))
 
-    @pl.when(jnp.logical_not(early))
+    @pl.when(between)
     def _():
-        wait_near()
+        pass_on(half_of[0])
 
     wait_far()
 
-    with jax.named_scope("pair_sums"):
-        lane = lax.broadcasted_iota(jnp.int32, (PANEL_ROWS, LANES), 1)
-        both = jnp.where(lane < LANES // 2, acc[:PANEL_ROWS, LANES:], acc[PANEL_ROWS:, LANES:])
-        groups = (PANEL_ROWS // OWN, OWN, LANES)
-        pair[:, 0] = acc[:PANEL_ROWS, :LANES].reshape(groups)
-        pair[:, 1] = acc[PANEL_ROWS:, :LANES].reshape(groups)
-        pair[:, 2] = both.reshape(groups)
-        to_pair = remote(pair.at[pl.ds(other * CHIPS, CHIPS)], sib, S_PAIR, sibling)
-        to_pair.start()
-
-        to_pair.wait_recv()
-        own = pl.ds(core * CHIPS, CHIPS)
-        red[...] = pair[own, 0:2] + sib[:, 0:2]
-        turned = (pair[own, 2] + sib[:, 2]).reshape(HALF, LANES).T
-        count[0] = turned[0:1, :]
-        count[1] = turned[LANES // 2:LANES // 2 + 1, :]
-
     with jax.named_scope("chip_sums"):
-        for i, (q, to) in enumerate(zip(chips, same_bin)):
-            remote(red.at[q], sums.at[i], S_SUMS, to).start()
-            remote(count, counts.at[i], S_COUNTS, to).start()
-
-        @pl.when(jnp.logical_not(early))
-        def _():
-            send_pieces()
-            pass_on(range(PIECES // 2))
+        own = pl.ds(pl.multiple_of(core * HALF, HALF), HALF)
+        diagonal = (lax.broadcasted_iota(jnp.int32, (HALF, LANES), 0)
+                    == lax.broadcasted_iota(jnp.int32, (HALF, LANES), 1))
+        for s in range(2):
+            to_pair[s].wait_recv()
+            red[s] = (acc[s, own, :LANES] + sib[s, :, :LANES]).reshape(CHIPS, OWN, LANES)
+            count[s] = jnp.sum(jnp.where(diagonal, acc[s, own, LANES:] + sib[s, :, LANES:], 0.0), axis=0, keepdims=True)
+            for i, (q, to) in enumerate(zip(chips, same_bin)):
+                remote(red.at[s, q], sums.at[s, i], S_SUMS + s, to).start()
+                if s:
+                    remote(count, counts.at[i], S_COUNTS, to).start()
+
+        @pl.when(late)
+        def _():
+            send_pieces(half_of[1])
+            pass_on(half_of[0])
+
+        @pl.when(jnp.logical_not(soon))
+        def _():
+            pass_on(half_of[1])
 
         for copy in small[2:]:
             copy.wait()
@@ -196,24 +199,23 @@
                   for s in range(2)]
         here = pl.ds(pl.multiple_of(core * HALF + chip * OWN, OWN), OWN)
         before = PRIOR * start[here, :]
-        wait(sums, recv_sem.at[S_SUMS])
-        total = red[chip]
+        wait(sums.at[0], recv_sem.at[S_SUMS])
+        total = red[0, chip]
         for i in range(CHIPS - 1):
-            total += sums[i]
-        middle = (total[0] + before) / weight[0]
-        cent[0, here, :] = (total[1] + PRIOR * middle) / weight[1]
+            total += sums[0, i]
+        middle = (total + before) / weight[0]
+        wait(sums.at[1], recv_sem.at[S_SUMS + 1])
+        total = red[1, chip]
+        for i in range(CHIPS - 1):
+            total += sums[1, i]
+        cent[0, here, :] = (total + PRIOR * middle) / weight[1]
 
     with jax.named_scope("gather_chips"):
         for i in range(CHIPS):
             remote(cent.at[0, here], cent.at[1, here], S_CENT, other_bin[i]).start()
             if i < CHIPS - 1:
                 remote(cent.at[0, here], cent.at[0, here], S_CENT, same_bin[i]).start()
-
-        @pl.when(jnp.logical_not(early))
-        def _():
-            pass_on(range(PIECES // 2, PIECES))
-
-        slices = acc.at[pl.ds(0, 2 * HALF - OWN), pl.ds(0, LANES)]
+        slices = acc.at[0, pl.ds(0, 2 * HALF - OWN), pl.ds(0, LANES)]
         wait(slices, recv_sem.at[S_CENT])
 
     with jax.named_scope("gather_cores"):
@@ -247,10 +249,12 @@
         wait(least.at[pl.ds(1, PANELS - 1)], recv_sem.at[S_LEAST])
         dist_out[...] = jnp.minimum(jnp.minimum(least[0], least[1]), jnp.minimum(least[2], least[3]))
 
-    to_pair.wait_send()
+    for copy in to_pair:
+        copy.wait_send()
     for copy in pieces:
         copy.wait_send()
-    wait(sums, send_sem.at[S_SUMS])
+    for s in range(2):
+        wait(sums.at[s], send_sem.at[S_SUMS + s])
     wait(counts, send_sem.at[S_COUNTS])
     wait(rows.at[pl.ds(0, (PANELS - 1) * QUARTER), pl.ds(LANES, LANES)], send_sem.at[S_ACROSS])
     wait(slices, send_sem.at[S_CENT])
@@ -274,11 +278,10 @@
             pltpu.VMEM((ROWS // LANES, LANES), jnp.int32),
             pltpu.VMEM((PANEL_ROWS, LANES), F32),
             pltpu.VMEM((OUT_ROWS, 2 * LANES), BF16),
-            pltpu.VMEM((2 * PANEL_ROWS, 2 * LANES), F32),
-            pltpu.VMEM((PANEL_ROWS // OWN, 3, OWN, LANES), F32),
-            pltpu.VMEM((CHIPS, 3, OWN, LANES), F32),
-            pltpu.VMEM((CHIPS, 2, OWN, LANES), F32),
-            pltpu.VMEM((CHIPS - 1, 2, OWN, LANES), F32),
+            pltpu.VMEM((2, PANEL_ROWS, 2 * LANES), F32),
+            pltpu.VMEM((2, HALF, 2 * LANES), F32),
+            pltpu.VMEM((2, CHIPS, OWN, LANES), F32),
+            pltpu.VMEM((2, CHIPS - 1, OWN, LANES), F32),
             pltpu.VMEM((2, 1, LANES), F32),
             pltpu.VMEM((CHIPS - 1, 2, 1, LANES), F32),
             pltpu.VMEM((2, PANEL_ROWS, LANES), F32),

time: 43.7 us -> 37.5 us (0.86)
  the two profiles are of different devices: /device:TPU:128 before, /device:TPU:1 now
where the time goes in v4:
time: 37.5 us; the launch traced here: 37.4 us
  Pallas kernels  35.5 us (95%)
  local copies, waits for them, and re-layouts  1.27 us (3%)
  between operations  0.64 us (2%)
    pallas_call x1, Pallas kernels, on_device(): pl.pallas_call(kernel, out_shape=(pltpu.VMEM((PANEL_ROWS, LANES), F32), p...  35.5 us
    unnamed x2, local copies, waits for them, and re-layouts  1.27 us

profile of v4, /device:TPU:1, one launch (start us, length us, event | category | flops | bytes accessed | tf_op | source)
XLA Modules:
  0.0 37.4 jit_solution(18092278897832121769)
XLA Ops:
  0.6 35.5 %shard_map.59 = (f32[256,128]{1,0:T(8,128)S(1)}, f32[1,6144]{1,0:T(1,128)S(1)}) custom-call(bf16[12288,128]{1,0:T(8,128)(2,1)} %hist.1, s32[96,128]{1,0:T(8,128)} %bitcast.4, s32[96,128]{1,0:T(8,128)} %bitcast.5, f32[256,128]{1,0:T(8,128)} %start_in.1), custom_call_target="tpu_custom_call" | custom-call | tf_op jit(solution)/shard_map/pallas_call | solution.py:270
  36.2 0.7 %copy.8 = f32[256,128]{1,0:T(8,128)} copy(f32[256,128]{1,0:T(8,128)S(1)} %get-tuple-element.6) | data formatting | bytes 262144
  36.8 0.6 %copy.9 = f32[6144]{0:T(1024)} copy(f32[6144]{0:T(1024)S(1)} %bitcast.3) | data formatting | bytes 49152

commit v5 on v4

--- a/solution.py
+++ b/solution.py
@@ -19,8 +19,8 @@
 CHUNKS = (2048, 6144, 4096)
 TILE = 256
 QUARTER = OUT_ROWS // PANELS
-PIECES = 4
-SOON, MID = 2, 4
+PIECES = 8
+FIRST = 2
 PIECE = QUARTER // PIECES
 
 S_PAIR, S_SUMS, S_ACROSS, S_COUNTS, S_CENT, S_COPY, S_LEAST, S_PIECE = 0, 2, 4, 5, 6, 7, 8, 9
@@ -110,10 +110,6 @@
                      rows.at[pl.ds(quarter + i * PIECE, PIECE), pl.ds(LANES, LANES)], S_PIECE + i, other_bin[-1])
               for i in range(PIECES)]
 
-    def send_pieces(which):
-        for i in which:
-            pieces[i].start()
-
     def pass_on(which):
         for i in which:
             pieces[i].wait_recv()
@@ -121,16 +117,11 @@
             for to in across:
                 remote(at, at, S_ACROSS, to).start()
 
-    soon, late = z < SOON, z >= MID
-    between = jnp.logical_and(z >= SOON, z < MID)
-    half_of = range(PIECES // 2), range(PIECES // 2, PIECES)
-
     hv[:, LANES:] = jnp.ones((ROWS, LANES), BF16)
 
-    @pl.when(jnp.logical_not(late))
-    def _():
-        wait_near()
-        send_pieces(range(PIECES))
+    wait_near()
+    for copy in pieces:
+        copy.start()
 
     with jax.named_scope("local_sums"):
         bucket = lax.broadcasted_iota(jnp.int32, (PANEL_ROWS, LANES), 0).astype(F32).astype(BF16)
@@ -149,20 +140,7 @@
                 acc[s] = acc[s] + part if at else part
                 if at == begins[-1]:
                     to_pair[s].start()
-            if at == begins[0]:
-                @pl.when(late)
-                def _():
-                    wait_near()
-                    send_pieces(half_of[0])
-
-    @pl.when(soon)
-    def _():
-        pass_on(range(PIECES))
-
-    @pl.when(between)
-    def _():
-        pass_on(half_of[0])
-
+    pass_on(range(FIRST))
     wait_far()
 
     with jax.named_scope("chip_sums"):
@@ -178,15 +156,7 @@
                 if s:
                     remote(count, counts.at[i], S_COUNTS, to).start()
 
-        @pl.when(late)
-        def _():
-            send_pieces(half_of[1])
-            pass_on(half_of[0])
-
-        @pl.when(jnp.logical_not(soon))
-        def _():
-            pass_on(half_of[1])
-
+        pass_on(range(FIRST, PIECES))
         for copy in small[2:]:
             copy.wait()
         wait(counts, recv_sem.at[S_COUNTS])

time: 37.5 us -> 36.1 us (0.963)
  Pallas kernels: 35.5 us -> 34.1 us
    pallas_call x1, Pallas kernels: 35.5 us -> 34.1 us  [on_device(): pl.pallas_call(kernel, out_shape=(pltpu.VMEM((PANEL_ROWS, LANES), F32), p...]
where the time goes in v5:
time: 36.1 us; the launch traced here: 36 us
  Pallas kernels  34.1 us (94%)
  local copies, waits for them, and re-layouts  1.27 us (4%)
  between operations  0.64 us (2%)
    pallas_call x1, Pallas kernels, on_device(): pl.pallas_call(kernel, out_shape=(pltpu.VMEM((PANEL_ROWS, LANES), F32), p...  34.1 us
    unnamed x2, local copies, waits for them, and re-layouts  1.27 us

profile of v5, /device:TPU:1, one launch (start us, length us, event | category | flops | bytes accessed | tf_op | source)
XLA Modules:
  0.0 36.0 jit_solution(14433598925975773855)
XLA Ops:
  0.6 34.1 %shard_map.59 = (f32[256,128]{1,0:T(8,128)S(1)}, f32[1,6144]{1,0:T(1,128)S(1)}) custom-call(bf16[12288,128]{1,0:T(8,128)(2,1)} %hist.1, s32[96,128]{1,0:T(8,128)} %bitcast.4, s32[96,128]{1,0:T(8,128)} %bitcast.5, f32[256,128]{1,0:T(8,128)} %start_in.1), custom_call_target="tpu_custom_call" | custom-call | tf_op jit(solution)/shard_map/pallas_call | solution.py:240
  34.7 0.7 %copy.8 = f32[256,128]{1,0:T(8,128)} copy(f32[256,128]{1,0:T(8,128)S(1)} %get-tuple-element.6) | data formatting | bytes 262144
  35.4 0.6 %copy.9 = f32[6144]{0:T(1024)} copy(f32[6144]{0:T(1024)S(1)} %bitcast.3) | data formatting | bytes 49152

commit v6 on v5

--- a/solution.py
+++ b/solution.py
@@ -23,7 +23,7 @@
 FIRST = 2
 PIECE = QUARTER // PIECES
 
-S_PAIR, S_SUMS, S_ACROSS, S_COUNTS, S_CENT, S_COPY, S_LEAST, S_PIECE = 0, 2, 4, 5, 6, 7, 8, 9
+S_PAIR, S_SUMS, S_CENT, S_COPY, S_ACROSS, S_COUNTS, S_LEAST, S_PIECE = 0, 2, 4, 6, 8, 9, 10, 11
 N_SEM = S_PIECE + PIECES
 
 
@@ -181,18 +181,19 @@
         cent[0, here, :] = (total + PRIOR * middle) / weight[1]
 
     with jax.named_scope("gather_chips"):
-        for i in range(CHIPS):
-            remote(cent.at[0, here], cent.at[1, here], S_CENT, other_bin[i]).start()
-            if i < CHIPS - 1:
-                remote(cent.at[0, here], cent.at[0, here], S_CENT, same_bin[i]).start()
-        slices = acc.at[0, pl.ds(0, 2 * HALF - OWN), pl.ds(0, LANES)]
-        wait(slices, recv_sem.at[S_CENT])
+        for to in same_bin:
+            remote(cent.at[0, here], cent.at[0, here], S_CENT, to).start()
+        for to in other_bin:
+            remote(cent.at[0, here], cent.at[1, here], S_CENT + 1, to).start()
+        slices = [acc.at[0, pl.ds(0, HALF - OWN), pl.ds(0, LANES)], acc.at[0, pl.ds(0, HALF), pl.ds(0, LANES)]]
 
     with jax.named_scope("gather_cores"):
         mine = pl.ds(pl.multiple_of(core * HALF, HALF), HALF)
         theirs = pl.ds(pl.multiple_of(other * HALF, HALF), HALF)
-        to_copy = remote(cent.at[:, mine], cent.at[:, mine], S_COPY, sibling)
-        to_copy.start()
+        to_copy = [remote(cent.at[b, mine], cent.at[b, mine], S_COPY + b, sibling) for b in range(2)]
+        for b in range(2):
+            wait(slices[b], recv_sem.at[S_CENT + b])
+            to_copy[b].start()
 
         def prepare(at, buckets):
             value = jnp.concatenate([cent[0, at, :], cent[1, at, :]], axis=1)
@@ -201,7 +202,8 @@
 
         prepare(mine, slice(0, HALF))
         own_rows.wait()
-        to_copy.wait_recv()
+        for copy in to_copy:
+            copy.wait_recv()
         prepare(theirs, slice(HALF, PANEL_ROWS))
         wait(rows.at[pl.ds(0, (PANELS - 1) * QUARTER), pl.ds(LANES, LANES)], recv_sem.at[S_ACROSS])
 
@@ -227,8 +229,9 @@
         wait(sums.at[s], send_sem.at[S_SUMS + s])
     wait(counts, send_sem.at[S_COUNTS])
     wait(rows.at[pl.ds(0, (PANELS - 1) * QUARTER), pl.ds(LANES, LANES)], send_sem.at[S_ACROSS])
-    wait(slices, send_sem.at[S_CENT])
-    to_copy.wait_send()
+    for b in range(2):
+        wait(slices[b], send_sem.at[S_CENT + b])
+        to_copy[b].wait_send()
     wait(least.at[pl.ds(1, PANELS - 1)], send_sem.at[S_LEAST])
 
 

time: 36.1 us -> 36.7 us (1.017)
  Pallas kernels: 34.1 us -> 34.7 us
    pallas_call x1, Pallas kernels: 34.1 us -> 34.7 us  [on_device(): pl.pallas_call(kernel, out_shape=(pltpu.VMEM((PANEL_ROWS, LANES), F32), p...]
where the time goes in v6:
time: 36.7 us
  Pallas kernels  34.7 us (95%)
  local copies, waits for them, and re-layouts  1.27 us (3%)
  between operations  0.64 us (2%)
    pallas_call x1, Pallas kernels, on_device(): pl.pallas_call(kernel, out_shape=(pltpu.VMEM((PANEL_ROWS, LANES), F32), p...  34.7 us
    unnamed x2, local copies, waits for them, and re-layouts  1.27 us

profile of v6, /device:TPU:1, one launch (start us, length us, event | category | flops | bytes accessed | tf_op | source)
XLA Modules:
  0.0 36.7 jit_solution(1621288596747125590)
XLA Ops:
  0.6 34.7 %shard_map.59 = (f32[256,128]{1,0:T(8,128)S(1)}, f32[1,6144]{1,0:T(1,128)S(1)}) custom-call(bf16[12288,128]{1,0:T(8,128)(2,1)} %hist.1, s32[96,128]{1,0:T(8,128)} %bitcast.4, s32[96,128]{1,0:T(8,128)} %bitcast.5, f32[256,128]{1,0:T(8,128)} %start_in.1), custom_call_target="tpu_custom_call" | custom-call | tf_op jit(solution)/shard_map/pallas_call | solution.py:243
  35.4 0.7 %copy.8 = f32[256,128]{1,0:T(8,128)} copy(f32[256,128]{1,0:T(8,128)S(1)} %get-tuple-element.6) | data formatting | bytes 262144
  36.0 0.6 %copy.9 = f32[6144]{0:T(1024)} copy(f32[6144]{0:T(1024)S(1)} %bitcast.3) | data formatting | bytes 49152
